TPU v7x, 32 devices: a whole 2x2x4 slice. The times are simulated.
32 devices in a mesh: flow: 8 (over y, x, core), cross: 4 (over z).
Axes of the slice: x: 2, y: 2, z: 4, core: 2. Of those that a mesh axis runs over, the one named last changes fastest.
Arguments:
- solid_temp: float32 [8, 2048, 2048], P(None, 'flow', 'cross'), may hold values from 0.5 to 1.5
- conductance: float32 [8, 2048, 2048], P(None, 'flow', 'cross'), may hold values from 0.03 to 0.12
- coolant: float32 [4, 2048, 2048], P(None, 'flow', 'cross'), may hold values from 0 to 1
- power_index: int32 [2048, 2048], P('flow', 'cross'), may hold values from 0 to 15
- power_levels: float32 [16], replicated, may hold values from 0.05 to 0.5
- channel_mask: int32 [4, 2048], P(None, 'cross'), may hold values 0 or 1
- inlet: float32 [4, 2048], P(None, 'cross'), may hold values from 0 to 0.5
- flow_gain: float32 [4, 2048], P(None, 'cross'), may hold values from 2 to 16
Outputs:
- solid_next: float32 [8, 2048, 2048], P(None, 'flow', 'cross')
- coolant_next: float32 [4, 2048, 2048], P(None, 'flow', 'cross')
All inputs are finite; a program needn't handle non-finite values. No bound on the sum of `channel_mask` on one device may be relied on, other than what follows from the above.
Results may differ from a plain program's by a relative error of at most 0.000058.
Values sent between devices are 32-bit elements; how exact they have to be, the bound alone decides.
A program may use at most 128 MiB of HBM per device.

v0:
```python
import functools

import jax
import jax.numpy as jnp
from jax import lax
from jax.experimental import pallas as pl
from jax.experimental.pallas import tpu as pltpu
from jax.sharding import PartitionSpec as P

MESH = pl.DeviceIdType.MESH
LANES = 128
CHUNK = 32
STEP = 32


def stencil(src, layer, start, size):
    count = src.shape[1]
    lane = lax.broadcasted_iota(jnp.int32, (size, LANES), 1)
    tiles = [src[layer, j, pl.ds(start + 8, size), :] for j in range(count)]
    none = jnp.zeros((size, LANES), jnp.float32)
    right_by_one = [none] + [pltpu.roll(t, 1, 1) for t in tiles]
    left_by_one = [pltpu.roll(t, LANES - 1, 1) for t in tiles] + [none]
    sums = []
    for j in range(count):
        left = jnp.where(lane == 0, right_by_one[j], right_by_one[j + 1])
        right = jnp.where(lane == LANES - 1, left_by_one[j + 1], left_by_one[j])
        above = src[layer, j, pl.ds(start + 7, size), :]
        below = src[layer, j, pl.ds(start + 9, size), :]
        sums.append((left + right) + (above + below))
    return jnp.concatenate(tiles, axis=1), jnp.concatenate(sums, axis=1)


def advance(src, cond, cool, film, heat, start, size, store):
    layers = src.shape[0]
    parts = [stencil(src, l, start, size) for l in range(layers)]
    rows = pl.ds(start, size)
    for l in range(layers):
        k = l // 2
        u, lateral = parts[l]
        near = [parts[m][0] for m in (l - 1, l + 1) if 0 <= m < layers]
        keep = (1.0 - 0.05 * len(near)) - film[k : k + 1, :]
        new = u * keep + cond[l, rows, :] * (lateral - 4.0 * u)
        new = new + 0.05 * (near[0] + near[1] if len(near) == 2 else near[0])
        new = new + film[k : k + 1, :] * cool[k, rows, :]
        if l == 0:
            new = new + heat
        store(l, new)


def pick(index, levels, count):
    values = [levels[i] for i in range(count)]
    bit = 1
    while len(values) > 1:
        if len(values) % 2:
            values.append(values[-1])
        odd = (index & bit) != 0
        values = [jnp.where(odd, values[i + 1], values[i]) for i in range(0, len(values), 2)]
        bit *= 2
    return values[0]


def kernel(
    n_flow, n_cross,
    u_hbm, c_hbm, cool_hbm, idx_hbm, lev_hbm, mask_hbm, inlet_hbm, gain_hbm,
    out, fluid, ends,
    u0, u1, cond, cool, idx, heat, lev, mask, inlet, gain,
    row_out, col_out, row_in, col_in, tot_out, tot_in,
    u_sem, big_sem, small_sem, halo_send, halo_recv, tot_send, tot_recv,
):
    layers, rows, width = u_hbm.shape
    chans = cool_hbm.shape[0]
    blocks = rows // 8
    per = LANES // layers
    groups = 4 if rows % (4 * STEP) == 0 else 1
    span = rows // groups
    lane_tiles = width // LANES
    edge_tiles = (0, lane_tiles - 1)
    me_f, me_c = lax.axis_index("flow"), lax.axis_index("cross")

    def loads(g):
        part = pl.ds(g * span, span)
        return [
            pltpu.make_async_copy(c_hbm.at[:, part], cond.at[:, part], big_sem.at[g, 1]),
            pltpu.make_async_copy(cool_hbm.at[:, part], cool.at[:, part], big_sem.at[g, 2]),
            pltpu.make_async_copy(idx_hbm.at[part], idx.at[part], big_sem.at[g, 3]),
        ]

    def load_u(g):
        return [
            pltpu.make_async_copy(
                u_hbm.at[:, pl.ds(g * span, span), pl.ds(j * LANES, LANES)],
                u0.at[:, j, pl.ds(8 + g * span, span)],
                u_sem.at[g, j],
            )
            for j in range(lane_tiles)
        ]

    small = [
        pltpu.make_async_copy(src, dst, small_sem.at[i])
        for i, (src, dst) in enumerate(
            [(lev_hbm, lev), (mask_hbm, mask), (inlet_hbm, inlet), (gain_hbm, gain)]
        )
    ]
    for g in range(groups):
        for one in load_u(g):
            one.start()
    for s in small:
        s.start()
    for g in range(groups):
        for one in loads(g):
            one.start()

    barrier = pltpu.get_barrier_semaphore()
    for d in range(1, n_flow):
        pl.semaphore_signal(
            barrier, inc=1, device_id=(lax.rem(me_f + d, n_flow), me_c), device_id_type=MESH
        )

    @pl.when(me_c > 0)
    def _():
        pl.semaphore_signal(barrier, inc=1, device_id=(me_f, me_c - 1), device_id_type=MESH)

    @pl.when(me_c < n_cross - 1)
    def _():
        pl.semaphore_signal(barrier, inc=1, device_id=(me_f, me_c + 1), device_id_type=MESH)

    zeros = jnp.zeros((layers, lane_tiles, 8, LANES), jnp.float32)
    for ref in (u0, u1):
        ref[:, :, 0:8, :] = zeros
        ref[:, :, rows + 8 : rows + 16, :] = zeros
    col_out[...] = jnp.zeros_like(col_out)
    tot_out[...] = jnp.zeros_like(tot_out)

    has = [me_f > 0, me_f < n_flow - 1, me_c > 0, me_c < n_cross - 1]
    peer = [
        (jnp.maximum(me_f - 1, 0), me_c),
        (jnp.minimum(me_f + 1, n_flow - 1), me_c),
        (me_f, jnp.maximum(me_c - 1, 0)),
        (me_f, jnp.minimum(me_c + 1, n_cross - 1)),
    ]

    def halo(turn, d):
        send, recv = (row_out, row_in) if d < 2 else (col_out, col_in)
        return pltpu.make_async_remote_copy(
            src_ref=send.at[turn, d % 2],
            dst_ref=recv.at[turn, 1 - d % 2],
            send_sem=halo_send.at[turn, d],
            recv_sem=halo_recv.at[turn, d + 1 - 2 * (d % 2)],
            device_id=peer[d],
            device_id_type=MESH,
        )

    def arrival(turn, d):
        recv = row_in if d < 2 else col_in
        return pltpu.make_async_remote_copy(
            src_ref=recv.at[turn, d % 2],
            dst_ref=recv.at[turn, d % 2],
            send_sem=halo_send.at[turn, d],
            recv_sem=halo_recv.at[turn, d],
            device_id=peer[d],
            device_id_type=MESH,
        )

    def send_halos(turn):
        for d in (2, 3, 0, 1):
            @pl.when(has[d])
            def _():
                halo(turn, d).start()

    def take_halos(turn):
        for d in range(4):
            @pl.when(has[d])
            def _():
                arrival(turn, d).wait_recv()

            @pl.when(jnp.logical_not(has[d]))
            def _():
                recv = row_in if d < 2 else col_in
                recv[turn, d % 2] = jnp.zeros(recv.shape[2:], jnp.float32)

    lane = lax.broadcasted_iota(jnp.int32, (8, LANES), 1)
    group = min(per, blocks)
    edge_cols = (pl.ds(0, LANES), pl.ds(width - LANES, LANES))
    is_layer = [lax.rem(lane, layers) == l for l in range(layers)]
    is_block = [lane // layers == i for i in range(group)]

    def turned(tile, shift):
        return pltpu.roll(tile, shift % LANES, 1) if shift % LANES else tile

    def pack_cols(turn, v, side, tile_of):
        packed = jnp.zeros((8, LANES), jnp.float32)
        for i in range(group):
            joined = jnp.zeros((8, LANES), jnp.float32)
            for l in range(layers):
                joined = jnp.where(is_layer[l], turned(tile_of(i, l), i * layers + l + side), joined)
            packed = jnp.where(is_block[i], joined, packed)
        col_out[turn, side, pl.ds(pl.multiple_of(v * 8, 8), 8), :] = packed

    def fix_cols(turn, v, side, view):
        target = side * (LANES - 1)
        packed = col_in[turn, side, pl.ds(pl.multiple_of(v * 8, 8), 8), :]
        edge = lane == target
        tiles = {}
        for i in range(group):
            at = pl.multiple_of((v * group + i) * 8, 8)
            for l in range(layers):
                beyond = jnp.where(edge, turned(packed, target - i * layers - l), 0.0)
                ref, where = view(side, l, at)
                tile = ref[where] + beyond * cond[l, pl.ds(at, 8), edge_cols[side]]
                ref[where] = tile
                tiles[i, l] = tile
        return lambda i, l: tiles[i, l]

    def lane_tile(j):
        return pl.ds(j * LANES, LANES)

    def in_u1(side, l, at):
        return u1, (l, edge_tiles[side], pl.ds(at + 8, 8), slice(None))

    def in_out(side, l, at):
        return out, (l, pl.ds(at, 8), edge_cols[side])

    def beyond_rows(turn, l, side, row, j):
        return (
            cond[l, pl.ds(row, 1), lane_tile(j)] * row_in[turn, side, pl.ds(l, 1), lane_tile(j)]
        )

    def fix_rows(turn, final):
        for l in range(layers):
            for side, row in ((0, 0), (1, rows - 1)):
                for j in range(lane_tiles):
                    term = beyond_rows(turn, l, side, row, j)
                    if final:
                        where = (l, pl.ds(row, 1), lane_tile(j))
                        out[where] = out[where] + term
                    else:
                        where = (l, j, pl.ds(row + 8, 1), slice(None))
                        u1[where] = u1[where] + term

    def pack_rows(turn, ref):
        for l in range(layers):
            for j in range(lane_tiles):
                for side, row in ((0, 8), (1, rows + 7)):
                    row_out[turn, side, pl.ds(l, 1), lane_tile(j)] = ref[l, j, pl.ds(row, 1), :]

    for g in range(groups):
        for one in load_u(g):
            one.wait()

    def pack_first(v, _):
        for side in range(2):
            pack_cols(
                0, v, side,
                lambda i, l: u0[
                    l,
                    edge_tiles[side],
                    pl.ds(pl.multiple_of((v * group + i) * 8 + 8, 8), 8),
                    :,
                ],
            )
        return 0

    lax.fori_loop(0, blocks // group, pack_first, 0)
    pack_rows(0, u0)
    pl.semaphore_wait(barrier, n_flow - 1 + has[2].astype(jnp.int32) + has[3].astype(jnp.int32))
    send_halos(0)

    for s in small:
        s.wait()
    film = 0.08 * mask[...].astype(jnp.float32)

    for g in range(groups):
        for one in loads(g):
            one.wait()

        def first(i, _):
            start = pl.multiple_of(g * span + i * STEP, STEP)
            warm = pick(idx[pl.ds(start, STEP), :], lev, lev.shape[0])
            heat[pl.ds(start, STEP), :] = warm

            def store(l, new):
                for j in range(lane_tiles):
                    u1[l, j, pl.ds(start + 8, STEP), :] = new[:, j * LANES : (j + 1) * LANES]

            advance(u0, cond, cool, film, warm, start, STEP, store)
            return 0

        lax.fori_loop(0, span // STEP, first, 0)

    take_halos(0)
    fix_rows(0, False)

    def fix_first(v, _):
        for side in range(2):
            pack_cols(1, v, side, fix_cols(0, v, side, in_u1))
        return 0

    lax.fori_loop(0, blocks // group, fix_first, 0)
    pack_rows(1, u1)
    send_halos(1)

    def second(i, _):
        start = pl.multiple_of(i * STEP, STEP)

        def store(l, new):
            out[l, pl.ds(start, STEP), :] = new

        advance(u1, cond, cool, film, heat[pl.ds(start, STEP), :], start, STEP, store)
        return 0

    lax.fori_loop(0, rows // STEP, second, 0)
    take_halos(1)
    fix_rows(1, True)

    def fix_second(v, _):
        for side in range(2):
            fix_cols(1, v, side, in_out)
        return 0

    lax.fori_loop(0, blocks // group, fix_second, 0)

    def take_up(i, sums):
        at = pl.ds(pl.multiple_of(i * CHUNK, CHUNK), CHUNK)
        new = []
        for k in range(chans):
            taken = film[k : k + 1, :] * (
                out[2 * k, at, :] + out[2 * k + 1, at, :] - 2.0 * cool[k, at, :]
            )
            fluid[k, at, :] = taken
            total = sums[k]
            for s in range(0, CHUNK, 8):
                total = total + taken[s : s + 8]
            new.append(total)
        return tuple(new)

    sums = lax.fori_loop(
        0, rows // CHUNK, take_up,
        tuple(jnp.zeros((8, width), jnp.float32) for _ in range(chans)),
    )
    for k in range(chans):
        tot_out[pl.ds(k, 1), :] = jnp.sum(sums[k], axis=0, keepdims=True)

    def carry(d):
        return pltpu.make_async_remote_copy(
            src_ref=tot_out,
            dst_ref=tot_in.at[d - 1],
            send_sem=tot_send.at[d - 1],
            recv_sem=tot_recv.at[d - 1],
            device_id=(lax.rem(me_f + d, n_flow), me_c),
            device_id_type=MESH,
        )

    for d in range(1, n_flow):
        @pl.when(me_f + d < n_flow)
        def _():
            carry(d).start()

    i_pos = lax.broadcasted_iota(jnp.int32, (rows, rows), 0)
    j_pos = lax.broadcasted_iota(jnp.int32, (rows, rows), 1)
    triangle = jnp.where(j_pos < i_pos, 1.0, jnp.where(j_pos == i_pos, 0.5, 0.0)).astype(
        jnp.bfloat16
    )
    part = 2 * LANES if width % (2 * LANES) == 0 else LANES
    for k in range(chans):
        for j in range(0, width, part):
            cols = pl.ds(j, part)
            taken = fluid[k, :, cols]
            high = taken.astype(jnp.bfloat16)
            low = (taken - high.astype(jnp.float32)).astype(jnp.bfloat16)
            fluid[k, :, cols] = jnp.dot(
                triangle, high, preferred_element_type=jnp.float32
            ) + jnp.dot(triangle, low, preferred_element_type=jnp.float32)

    for d in range(1, n_flow):
        @pl.when(me_f >= d)
        def _():
            carry(d).wait_recv()

        @pl.when(me_f < d)
        def _():
            tot_in[d - 1] = jnp.zeros(tot_in.shape[1:], jnp.float32)

    carried = tot_in[0]
    for d in range(2, n_flow):
        carried = carried + tot_in[d - 1]
    scale = gain[...] * (1.0 / (rows * n_flow))
    ends[0] = inlet[...] + scale * carried[:chans]
    ends[1] = scale

    for turn in range(2):
        for d in range(4):
            @pl.when(has[d])
            def _():
                halo(turn, d).wait_send()
    for d in range(1, n_flow):
        @pl.when(me_f + d < n_flow)
        def _():
            carry(d).wait_send()


def finish(solid, within, ends, out, fluid, held, solid_sem, fluid_sem):
    chans, rows, _ = within.shape
    whole = pltpu.make_async_copy(solid, out, solid_sem)
    whole.start()
    parts = []
    for k in range(chans):
        def march(i, _):
            at = pl.ds(pl.multiple_of(i * STEP, STEP), STEP)
            held[k, at, :] = ends[0, k : k + 1, :] + ends[1, k : k + 1, :] * within[k, at, :]
            return 0

        lax.fori_loop(0, rows // STEP, march, 0)
        parts.append(pltpu.make_async_copy(held.at[k], fluid.at[k], fluid_sem.at[k]))
        parts[k].start()
    whole.wait()
    for part in parts:
        part.wait()


def shards(
    solid_temp, conductance, coolant, power_index, power_levels, channel_mask, inlet, flow_gain
):
    n_flow, n_cross = lax.axis_size("flow"), lax.axis_size("cross")
    layers, rows, width = solid_temp.shape
    chans = coolant.shape[0]
    f32 = jnp.float32
    packed = pl.cdiv(rows // 8, LANES // layers) * 8
    totals = pl.cdiv(chans, 8) * 8
    scratch = [
        pltpu.VMEM((layers, width // LANES, rows + 16, LANES), f32),
        pltpu.VMEM((layers, width // LANES, rows + 16, LANES), f32),
        pltpu.VMEM((layers, rows, width), f32),
        pltpu.VMEM((chans, rows, width), f32),
        pltpu.VMEM((rows, width), jnp.int32),
        pltpu.VMEM((rows, width), f32),
        pltpu.SMEM(power_levels.shape, f32),
        pltpu.VMEM((chans, width), jnp.int32),
        pltpu.VMEM((chans, width), f32),
        pltpu.VMEM((chans, width), f32),
        pltpu.VMEM((2, 2, layers, width), f32),
        pltpu.VMEM((2, 2, packed, LANES), f32),
        pltpu.VMEM((2, 2, layers, width), f32),
        pltpu.VMEM((2, 2, packed, LANES), f32),
        pltpu.VMEM((totals, width), f32),
        pltpu.VMEM((n_flow - 1, totals, width), f32),
        pltpu.SemaphoreType.DMA((4, width // LANES)),
        pltpu.SemaphoreType.DMA((4, 4)),
        pltpu.SemaphoreType.DMA((4,)),
        pltpu.SemaphoreType.DMA((2, 4)),
        pltpu.SemaphoreType.DMA((2, 4)),
        pltpu.SemaphoreType.DMA((n_flow - 1,)),
        pltpu.SemaphoreType.DMA((n_flow - 1,)),
    ]
    cells = layers * rows * width
    limit = 57 * 1024 * 1024
    solid, within, ends = pl.pallas_call(
        functools.partial(kernel, n_flow, n_cross),
        out_shape=(
            pltpu.VMEM((layers, rows, width), f32),
            pltpu.VMEM((chans, rows, width), f32),
            pltpu.VMEM((2, chans, width), f32),
        ),
        in_specs=[pl.BlockSpec(memory_space=pltpu.HBM)] * 8,
        out_specs=(pl.BlockSpec(memory_space=pltpu.VMEM),) * 3,
        scratch_shapes=scratch,
        compiler_params=pltpu.CompilerParams(
            collective_id=0, has_side_effects=True, vmem_limit_bytes=limit
        ),
        cost_estimate=pl.CostEstimate(
            flops=40 * cells, bytes_accessed=11 * cells, transcendentals=0
        ),
    )(
        solid_temp, conductance, coolant, power_index, power_levels, channel_mask, inlet, flow_gain
    )
    return pl.pallas_call(
        finish,
        out_shape=(
            jax.ShapeDtypeStruct((layers, rows, width), f32),
            jax.ShapeDtypeStruct((chans, rows, width), f32),
        ),
        in_specs=[pl.BlockSpec(memory_space=pltpu.VMEM)] * 3,
        out_specs=(pl.BlockSpec(memory_space=pltpu.HBM),) * 2,
        scratch_shapes=[
            pltpu.VMEM((chans, rows, width), f32),
            pltpu.SemaphoreType.DMA,
            pltpu.SemaphoreType.DMA((chans,)),
        ],
        compiler_params=pltpu.CompilerParams(vmem_limit_bytes=16 * 1024 * 1024),
        cost_estimate=pl.CostEstimate(flops=cells, bytes_accessed=6 * cells, transcendentals=0),
    )(solid, within, ends)


def solution(mesh):
    return jax.shard_map(
        shards,
        mesh=mesh,
        in_specs=(
            P(None, "flow", "cross"),
            P(None, "flow", "cross"),
            P(None, "flow", "cross"),
            P("flow", "cross"),
            P(),
            P(None, "cross"),
            P(None, "cross"),
            P(None, "cross"),
        ),
        out_specs=(P(None, "flow", "cross"), P(None, "flow", "cross")),
        check_vma=False,
    )
```

profile of v0, /device:TPU:13, one launch (start us, length us, event | category | flops | bytes accessed | tf_op | source)
XLA Modules:
  0.0 20.6 jit_solution(14012971216426484982)
XLA Ops:
  0.6 17.3 %shard_map.95 = (f32[8,256,512]{2,1,0:T(8,128)S(1)}, f32[4,256,512]{2,1,0:T(8,128)S(1)}, f32[2,4,512]{2,1,0:T(4,128)S(1)}) custom-call(f32[8,256,512]{2,1,0:T(8,128)} %u_hbm.1, f32[8,256,512]{2,1,0:T(8,128)} %c_hbm.1, f32[4,256,512]{2,1,0:T(8,128)} %cool_hbm.1, s32[256,512]{1,0:T(8,128)} %idx_hbm.1, f32[16]{0:T(128)} %lev_hbm.1, s32[4,512]{1,0:T(4,128)} %mask_hbm.1, ...), custom_call_target="tpu_custom_call" | custom-call | flops 41943040 | bytes 11534336 | tf_op jit(solution)/shard_map/pallas_call | solution.py:456
  17.9 2.7 %shard_map.96 = (f32[8,256,512]{2,1,0:T(8,128)}, f32[4,256,512]{2,1,0:T(8,128)}) custom-call(f32[8,256,512]{2,1,0:T(8,128)S(1)} %get-tuple-element.5.solid, f32[4,256,512]{2,1,0:T(8,128)S(1)} %get-tuple-element.6.within, f32[2,4,512]{2,1,0:T(4,128)S(1)} %get-tuple-element.7.ends), custom_call_target="tpu_custom_call" | custom-call | flops 1048576 | bytes 6291456 | tf_op jit(solution)/shard_map/pallas_call | solution.py:475
where the time goes:
time: 20.7 us; the launch traced here: 20.6 us
  Pallas kernels  20 us (97%)
  between operations  0.64 us (3%)
    pallas_call x1, Pallas kernels, shards(): pl.pallas_call(functools.partial(kernel, n_flow, n_cross), out_shape=(plt...  17.3 us
    pallas_call x1, Pallas kernels, shards(): pl.pallas_call(finish, out_shape=(jax.ShapeDtypeStruct((layers, rows, wid...  2.69 us

commit v1 on v0

--- a/solution.py
+++ b/solution.py
@@ -13,10 +13,9 @@
 STEP = 32
 
 
-def stencil(src, layer, start, size):
-    count = src.shape[1]
+def lateral_sum(src, layer, tiles, start, size):
+    count = len(tiles)
     lane = lax.broadcasted_iota(jnp.int32, (size, LANES), 1)
-    tiles = [src[layer, j, pl.ds(start + 8, size), :] for j in range(count)]
     none = jnp.zeros((size, LANES), jnp.float32)
     right_by_one = [none] + [pltpu.roll(t, 1, 1) for t in tiles]
     left_by_one = [pltpu.roll(t, LANES - 1, 1) for t in tiles] + [none]
@@ -27,24 +26,35 @@
         above = src[layer, j, pl.ds(start + 7, size), :]
         below = src[layer, j, pl.ds(start + 9, size), :]
         sums.append((left + right) + (above + below))
-    return jnp.concatenate(tiles, axis=1), jnp.concatenate(sums, axis=1)
+    return jnp.concatenate(sums, axis=1)
 
 
 def advance(src, cond, cool, film, heat, start, size, store):
-    layers = src.shape[0]
-    parts = [stencil(src, l, start, size) for l in range(layers)]
+    layers, count = src.shape[:2]
     rows = pl.ds(start, size)
+
+    def tiles_of(l):
+        if not 0 <= l < layers:
+            return None
+        return [src[l, j, pl.ds(start + 8, size), :] for j in range(count)]
+
+    below, tiles, above = None, tiles_of(0), tiles_of(1)
+    supply = None
     for l in range(layers):
         k = l // 2
-        u, lateral = parts[l]
-        near = [parts[m][0] for m in (l - 1, l + 1) if 0 <= m < layers]
+        u = jnp.concatenate(tiles, axis=1)
+        near = [jnp.concatenate(t, axis=1) for t in (below, above) if t is not None]
+        if l % 2 == 0:
+            supply = film[k : k + 1, :] * cool[k, rows, :]
         keep = (1.0 - 0.05 * len(near)) - film[k : k + 1, :]
+        lateral = lateral_sum(src, l, tiles, start, size)
         new = u * keep + cond[l, rows, :] * (lateral - 4.0 * u)
         new = new + 0.05 * (near[0] + near[1] if len(near) == 2 else near[0])
-        new = new + film[k : k + 1, :] * cool[k, rows, :]
+        new = new + supply
         if l == 0:
             new = new + heat
         store(l, new)
+        below, tiles, above = tiles, above, tiles_of(l + 2)
 
 
 def pick(index, levels, count):
@@ -187,12 +197,12 @@
     def turned(tile, shift):
         return pltpu.roll(tile, shift % LANES, 1) if shift % LANES else tile
 
-    def pack_cols(turn, v, side, tile_of):
+    def pack_cols(turn, v, side, tiles_of):
         packed = jnp.zeros((8, LANES), jnp.float32)
         for i in range(group):
             joined = jnp.zeros((8, LANES), jnp.float32)
-            for l in range(layers):
-                joined = jnp.where(is_layer[l], turned(tile_of(i, l), i * layers + l + side), joined)
+            for l, tile in enumerate(tiles_of(i)):
+                joined = jnp.where(is_layer[l], turned(tile, i * layers + l + side), joined)
             packed = jnp.where(is_block[i], joined, packed)
         col_out[turn, side, pl.ds(pl.multiple_of(v * 8, 8), 8), :] = packed
 
@@ -200,16 +210,20 @@
         target = side * (LANES - 1)
         packed = col_in[turn, side, pl.ds(pl.multiple_of(v * 8, 8), 8), :]
         edge = lane == target
-        tiles = {}
-        for i in range(group):
+
+        def fixed(i):
             at = pl.multiple_of((v * group + i) * 8, 8)
+            tiles = []
             for l in range(layers):
                 beyond = jnp.where(edge, turned(packed, target - i * layers - l), 0.0)
                 ref, where = view(side, l, at)
-                tile = ref[where] + beyond * cond[l, pl.ds(at, 8), edge_cols[side]]
-                ref[where] = tile
-                tiles[i, l] = tile
-        return lambda i, l: tiles[i, l]
+                tiles.append(ref[where] + beyond * cond[l, pl.ds(at, 8), edge_cols[side]])
+            for l in range(layers):
+                ref, where = view(side, l, at)
+                ref[where] = tiles[l]
+            return tiles
+
+        return fixed
 
     def lane_tile(j):
         return pl.ds(j * LANES, LANES)
@@ -226,16 +240,17 @@
         )
 
     def fix_rows(turn, final):
-        for l in range(layers):
-            for side, row in ((0, 0), (1, rows - 1)):
+        for side, row in ((0, 0), (1, rows - 1)):
+            done = []
+            for l in range(layers):
                 for j in range(lane_tiles):
-                    term = beyond_rows(turn, l, side, row, j)
                     if final:
-                        where = (l, pl.ds(row, 1), lane_tile(j))
-                        out[where] = out[where] + term
+                        ref, where = out, (l, pl.ds(row, 1), lane_tile(j))
                     else:
-                        where = (l, j, pl.ds(row + 8, 1), slice(None))
-                        u1[where] = u1[where] + term
+                        ref, where = u1, (l, j, pl.ds(row + 8, 1), slice(None))
+                    done.append((ref, where, ref[where] + beyond_rows(turn, l, side, row, j)))
+            for ref, where, value in done:
+                ref[where] = value
 
     def pack_rows(turn, ref):
         for l in range(layers):
@@ -243,24 +258,20 @@
                 for side, row in ((0, 8), (1, rows + 7)):
                     row_out[turn, side, pl.ds(l, 1), lane_tile(j)] = ref[l, j, pl.ds(row, 1), :]
 
-    for g in range(groups):
-        for one in load_u(g):
-            one.wait()
-
-    def pack_first(v, _):
+    arrived = 0
+    for v in range(blocks // group):
+        while arrived * span < (v + 1) * group * 8:
+            for one in load_u(arrived):
+                one.wait()
+            arrived += 1
         for side in range(2):
             pack_cols(
                 0, v, side,
-                lambda i, l: u0[
-                    l,
-                    edge_tiles[side],
-                    pl.ds(pl.multiple_of((v * group + i) * 8 + 8, 8), 8),
-                    :,
+                lambda i: [
+                    u0[l, edge_tiles[side], pl.ds((v * group + i) * 8 + 8, 8), :]
+                    for l in range(layers)
                 ],
             )
-        return 0
-
-    lax.fori_loop(0, blocks // group, pack_first, 0)
     pack_rows(0, u0)
     pl.semaphore_wait(barrier, n_flow - 1 + has[2].astype(jnp.int32) + has[3].astype(jnp.int32))
     send_halos(0)
@@ -274,15 +285,16 @@
             one.wait()
 
         def first(i, _):
-            start = pl.multiple_of(g * span + i * STEP, STEP)
-            warm = pick(idx[pl.ds(start, STEP), :], lev, lev.shape[0])
-            heat[pl.ds(start, STEP), :] = warm
-
-            def store(l, new):
-                for j in range(lane_tiles):
-                    u1[l, j, pl.ds(start + 8, STEP), :] = new[:, j * LANES : (j + 1) * LANES]
-
-            advance(u0, cond, cool, film, warm, start, STEP, store)
+            for sub in range(0, STEP, 8):
+                start = pl.multiple_of(g * span + i * STEP + sub, 8)
+                warm = pick(idx[pl.ds(start, 8), :], lev, lev.shape[0])
+                heat[pl.ds(start, 8), :] = warm
+
+                def store(l, new):
+                    for j in range(lane_tiles):
+                        u1[l, j, pl.ds(start + 8, 8), :] = new[:, j * LANES : (j + 1) * LANES]
+
+                advance(u0, cond, cool, film, warm, start, 8, store)
             return 0
 
         lax.fori_loop(0, span // STEP, first, 0)
@@ -300,12 +312,13 @@
     send_halos(1)
 
     def second(i, _):
-        start = pl.multiple_of(i * STEP, STEP)
-
-        def store(l, new):
-            out[l, pl.ds(start, STEP), :] = new
-
-        advance(u1, cond, cool, film, heat[pl.ds(start, STEP), :], start, STEP, store)
+        for sub in range(0, STEP, 8):
+            start = pl.multiple_of(i * STEP + sub, 8)
+
+            def store(l, new):
+                out[l, pl.ds(start, 8), :] = new
+
+            advance(u1, cond, cool, film, heat[pl.ds(start, 8), :], start, 8, store)
         return 0
 
     lax.fori_loop(0, rows // STEP, second, 0)
@@ -314,7 +327,9 @@
 
     def fix_second(v, _):
         for side in range(2):
-            fix_cols(1, v, side, in_out)
+            fixed = fix_cols(1, v, side, in_out)
+            for i in range(group):
+                fixed(i)
         return 0
 
     lax.fori_loop(0, blocks // group, fix_second, 0)

time: 20.7 us -> 23.3 us (1.13)
  Pallas kernels: 20 us -> 22.5 us
    pallas_call x1, Pallas kernels: 17.3 us -> 19.8 us  [shards(): pl.pallas_call(functools.partial(kernel, n_flow, n_cross), out_shape=(plt...]
where the time goes in v1:
time: 23.3 us; the launch traced here: 23.1 us
  Pallas kernels  22.5 us (97%)
  between operations  0.64 us (3%)
    pallas_call x1, Pallas kernels, shards(): pl.pallas_call(functools.partial(kernel, n_flow, n_cross), out_shape=(plt...  19.8 us
    pallas_call x1, Pallas kernels, shards(): pl.pallas_call(finish, out_shape=(jax.ShapeDtypeStruct((layers, rows, wid...  2.69 us

profile of v1, /device:TPU:13, one launch (start us, length us, event | category | flops | bytes accessed | tf_op | source)
XLA Modules:
  0.0 23.1 jit_solution(8937523227175571318)
XLA Ops:
  0.6 19.8 %shard_map.95 = (f32[8,256,512]{2,1,0:T(8,128)S(1)}, f32[4,256,512]{2,1,0:T(8,128)S(1)}, f32[2,4,512]{2,1,0:T(4,128)S(1)}) custom-call(f32[8,256,512]{2,1,0:T(8,128)} %u_hbm.1, f32[8,256,512]{2,1,0:T(8,128)} %c_hbm.1, f32[4,256,512]{2,1,0:T(8,128)} %cool_hbm.1, s32[256,512]{1,0:T(8,128)} %idx_hbm.1, f32[16]{0:T(128)} %lev_hbm.1, s32[4,512]{1,0:T(4,128)} %mask_hbm.1, ...), custom_call_target="tpu_custom_call" | custom-call | flops 41943040 | bytes 11534336 | tf_op jit(solution)/shard_map/pallas_call | solution.py:471
  20.4 2.7 %shard_map.96 = (f32[8,256,512]{2,1,0:T(8,128)}, f32[4,256,512]{2,1,0:T(8,128)}) custom-call(f32[8,256,512]{2,1,0:T(8,128)S(1)} %get-tuple-element.5.solid, f32[4,256,512]{2,1,0:T(8,128)S(1)} %get-tuple-element.6.within, f32[2,4,512]{2,1,0:T(4,128)S(1)} %get-tuple-element.7.ends), custom_call_target="tpu_custom_call" | custom-call | flops 1048576 | bytes 6291456 | tf_op jit(solution)/shard_map/pallas_call | solution.py:490
